TPU v7x, 32 devices: a whole 2x2x4 slice. The times are simulated.
32 devices in a mesh: energy: 8 (over y, x, core), slab: 4 (over z).
Axes of the slice: x: 2, y: 2, z: 4, core: 2. Of those that a mesh axis runs over, the one named last changes fastest.
Arguments:
- slab_counts: int32 [4], replicated, may hold values from 2 to 4, as said below
- energy_index: int32 [8], replicated, may hold values from 0 to 31, as said below
- hamiltonian_blocks: float32 [16, 128, 128], P('slab'), as said below
- couplings: float32 [16, 128, 128], P('slab'), as said below
- injection: float32 [8, 16, 128, 128], P('energy', 'slab'), may hold values from -6 to 6
Outputs:
- lesser: float32 [8, 16, 128, 128], P('energy', 'slab')
- self_energy: float32 [8, 16, 128, 128], P(None, 'slab', 'energy')
Inputs may be any that keep to these rules, and one draw needn't show every extreme that they name: `slab_counts`: each index holds 2 or more slabs, and some index holds exactly 4. `energy_index`: distinct and ascending; the first is 0 and the last 31. `hamiltonian_blocks`: symmetric; with the couplings, every operator M_e of the window is positive definite. `couplings`: with the Hamiltonian blocks, every operator M_e of the window is positive definite.
All inputs are finite; a program needn't handle non-finite values.
Results may differ from a plain program's by a relative error of at most 0.0003.
Values sent between devices are 32-bit elements; how exact they have to be, the bound alone decides.
A program may use at most 64 MiB of HBM per device.

v0:
```python
import functools
import jax
import jax.numpy as jnp
from jax import lax
from jax.experimental import pallas as pl
from jax.experimental.pallas import tpu as pltpu
from jax.sharding import PartitionSpec as P

HIGHEST = lax.Precision.HIGHEST
MESH = pl.DeviceIdType.MESH


def contract(left, right, a, b):
    return lax.dot_general(
        left, right, (((a,), (b,)), ((), ())), precision=HIGHEST, preferred_element_type=jnp.float32
    )


def nn(left, right):
    return contract(left, right, 1, 0)


def tn(left, right):
    return contract(left, right, 0, 0)


def nt(left, right):
    return contract(left, right, 1, 1)


def weighted(weights, rows):
    terms = [w * r for w, r in zip(weights, rows)]
    while len(terms) > 1:
        terms = [terms[i] + terms[i + 1] for i in range(0, len(terms), 2)]
    return terms[0]


def small_inverse(block):
    size = len(block)
    if size == 2:
        a, b, d = block[0][0], block[0][1], block[1][1]
        scale = 1.0 / (a * d - b * b)
        a, b, d = a * scale, b * scale, d * scale
        return lambda rows: [d * rows[0] - b * rows[1], a * rows[1] - b * rows[0]]
    h = size // 2
    first = small_inverse([r[:h] for r in block[:h]])
    columns = [[block[i][h + j] for i in range(h)] for j in range(h)]
    cross = [first(column) for column in columns]
    schur = [[None] * h for _ in range(h)]
    for i in range(h):
        for j in range(i, h):
            schur[i][j] = schur[j][i] = block[h + i][h + j] - weighted(columns[i], cross[j])
    second = small_inverse(schur)

    def apply(rows):
        upper = first(rows[:h])
        x2 = second([rows[h + i] - weighted(cross[i], rows[:h]) for i in range(h)])
        x1 = [upper[i] - weighted([cross[j][i] for j in range(h)], x2) for i in range(h)]
        return x1 + x2

    return apply


def sweep(chunks, k, size):
    lane = lax.broadcasted_iota(jnp.int32, (8, 128), 1)
    sub = lax.broadcasted_iota(jnp.int32, (8, 128), 0)
    at, o = k // 8, k % 8
    columns = [
        [jnp.broadcast_to(c[:, k + q : k + q + 1], (8, 128)) for c in chunks] for q in range(size)
    ]
    block = [[None] * size for _ in range(size)]
    for i in range(size):
        for j in range(i, size):
            block[i][j] = block[j][i] = columns[i][at][o + j : o + j + 1, :]
    inside = (lane >= k) & (lane < k + size)
    pivots = jnp.where(inside, jnp.where(lane - k == sub - o, -1.0, 0.0), chunks[at])
    solved = small_inverse(block)([pivots[o + i : o + i + 1, :] for i in range(size)])
    solved = [jnp.broadcast_to(x, (8, 128)) for x in solved]
    out = []
    for c in range(len(chunks)):
        change = weighted([columns[q][c] for q in range(size)], solved)
        value = jnp.where(inside, 0.0, chunks[c]) - change
        if c == at:
            for i in range(size):
                value = jnp.where(sub == o + i, solved[i], value)
        out.append(value)
    return out


def inverses(matrices):
    size, unroll = (8, 2) if len(matrices) == 1 else (4, 4)
    lane = lax.broadcasted_iota(jnp.int32, (8, 128), 1)
    sub = lax.broadcasted_iota(jnp.int32, (8, 128), 0)
    count = matrices[0].shape[0] // 8
    scales, sets = [], []
    for matrix in matrices:
        chunks = [matrix[8 * i : 8 * i + 8, :] for i in range(count)]
        top = jnp.zeros((8, 128), jnp.float32)
        for i in range(count):
            top = jnp.maximum(top, jnp.where(lane - sub == 8 * i, chunks[i], 0.0))
        scale = 1.0 / jnp.max(top, axis=(0, 1), keepdims=True)
        scales.append(scale)
        sets.append([c * scale for c in chunks])

    def body(_, carry):
        sets = [list(s) for s in carry]
        for k in range(0, 8 * unroll, size):
            sets = [sweep(s, k, size) for s in sets]
        return [
            [pltpu.roll(c, 128 - 8 * unroll, 1) for c in s[unroll:] + s[:unroll]] for s in sets
        ]

    sets = lax.fori_loop(0, count // unroll, body, sets)
    return [
        jnp.concatenate([c * -scale for c in s], axis=0) for s, scale in zip(sets, scales)
    ]


def kernel(
    ne, nslab, counts_in, energies_in, ham_in, link_in, inj_in, lesser, selfe,
    counts, energies, ham, link, inj, si,
    keep, out_a, in_a, out_b, in_b, out_c, in_c, out_d, in_d, out_e, in_e, weights,
    sa, ra, sb, rb, sc, rc, sd, rd, se, re,
):
    pairs = [
        (counts_in, counts), (energies_in, energies), (ham_in, ham), (link_in, link), (inj_in, inj)
    ]
    staged = [pltpu.make_async_copy(a, b, si.at[i]) for i, (a, b) in enumerate(pairs)]
    for copy in staged:
        copy.start()
    e = lax.axis_index("energy")
    p = lax.axis_index("slab")
    half = nslab // 2
    width = ham.shape[1]
    cap = ham.shape[0]
    rows = width // ne
    is_left = p < half
    is_outer = (p == 0) | (p == nslab - 1)
    is_middle = (p == half - 1) | (p == half)
    takes_a = (p > 0) & (p <= half)
    inward = jnp.where(is_left, p + 1, p - 1)
    outward = jnp.where(is_left, p - 1, p + 1)

    barrier = pltpu.get_barrier_semaphore()
    for i in range(1, ne):
        pl.semaphore_signal(
            barrier, inc=1, device_id=(lax.rem(e + i, ne), p), device_id_type=MESH
        )

    @pl.when(p > 0)
    def _():
        pl.semaphore_signal(barrier, inc=1, device_id=(e, p - 1), device_id_type=MESH)

    @pl.when(p < nslab - 1)
    def _():
        pl.semaphore_signal(barrier, inc=1, device_id=(e, p + 1), device_id_type=MESH)

    def send(src, dst, send_sem, recv_sem, to):
        return pltpu.make_async_remote_copy(
            src_ref=src, dst_ref=dst, send_sem=send_sem, recv_sem=recv_sem,
            device_id=(e, to), device_id_type=MESH,
        )

    for copy in staged:
        copy.wait()
    shape = (width, width)
    eye = (
        lax.broadcasted_iota(jnp.int32, shape, 0) == lax.broadcasted_iota(jnp.int32, shape, 1)
    ).astype(jnp.float32)
    shift = 0.02 + 0.06 * energies[e].astype(jnp.float32) / (4 * ne)
    shifted = eye * shift
    count = jnp.full(shape, counts[p], jnp.int32)
    two, three, four = count == 2, count >= 3, count == 4
    inner = jnp.full(shape, p, jnp.int32) < nslab - 1
    zero = jnp.zeros(shape, jnp.float32)

    diag_a = jnp.where(three, ham[1] + shifted, eye)
    diag_d = jnp.where(four, ham[3] + shifted, eye)
    inv_a, inv_d = inverses([diag_a, diag_d])
    link_0a = jnp.where(three, link[0], zero)
    link_0b = jnp.where(three, zero, link[0])
    link_ab = jnp.where(three, link[1], zero)
    link_bd = jnp.where(four, link[2], zero)
    link_dt = jnp.where(four & inner, link[3], zero)
    link_bt = jnp.where(inner, jnp.where(two, link[1], jnp.where(four, zero, link[2])), zero)
    rhs_a = jnp.where(three, inj[0, 1], zero)
    rhs_b = jnp.where(three, inj[0, 2], inj[0, 1])
    rhs_d = jnp.where(four, inj[0, 3], zero)
    diag_b = jnp.where(three, ham[2], ham[1]) + shifted

    xab = nn(inv_a, link_ab)
    xdb = nt(inv_d, link_bd)
    diag_b = diag_b - tn(link_ab, xab) - nn(link_bd, xdb)
    keep[2] = inv_a
    keep[3] = inv_d
    keep[4] = xab
    keep[6] = xdb
    (inv_b,) = inverses([diag_b])

    def send_a(i):
        return send(out_a.at[i], in_a.at[i], sa.at[i], ra.at[i], p + 1)

    def send_b(i):
        return send(out_b.at[i], in_b.at[i], sb.at[i], rb.at[i], inward)

    def send_c(i):
        return send(out_c.at[i], in_c.at[i], sc.at[i], rc.at[i], inward)

    def send_d():
        return send(out_d, in_d, sd, rd, outward)

    inv_a, inv_d, xab, xdb = keep[2], keep[3], keep[4], keep[6]
    link_0b = link_0b - nn(link_0a, xab)
    xa0 = nt(inv_a, link_0a)
    xb0 = nt(inv_b, link_0b)
    node = ham[0] + shifted - nn(link_0a, xa0) - nn(link_0b, xb0)
    keep[0] = node
    out_b[0] = node
    keep[2] = xa0
    keep[8] = xb0

    pl.semaphore_wait(barrier, ne - 1 + jnp.where(is_outer, 1, 2))

    @pl.when(p == nslab - 1)
    def _():
        send_b(0).start()

    xdt = nn(inv_d, link_dt)
    link_bt = link_bt - nn(link_bd, xdt)
    xbt = nn(inv_b, link_bt)
    out_a[0] = tn(link_dt, xdt) + tn(link_bt, xbt)
    keep[5] = xdt
    keep[9] = xbt

    @pl.when(is_left)
    def _():
        send_a(0).start()

    xaf = nn(inv_a, rhs_a)
    xdf = nn(inv_d, rhs_d)
    rhs_b = rhs_b - tn(link_ab, xaf) - nn(link_bd, xdf)
    xbf = nn(inv_b, rhs_b)
    node_rhs = inj[0, 0] - nn(link_0a, xaf) - nn(link_0b, xbf)
    keep[1] = node_rhs
    out_b[1] = node_rhs

    @pl.when(p == nslab - 1)
    def _():
        send_b(1).start()

    out_a[1] = tn(link_dt, xdf) + tn(link_bt, xbf)
    out_a[2] = -tn(link_bt, xb0)

    @pl.when(is_left)
    def _():
        send_a(1).start()

    @pl.when(p == half - 1)
    def _():
        send_a(2).start()

    own_link = -nn(link_0b, xbt)
    keep[3], keep[7], keep[10] = xaf, xdf, xbf
    keep[11] = own_link
    keep[12] = own_link

    @pl.when(jnp.logical_not(is_left) & jnp.logical_not(is_outer))
    def _():
        send_b(0).wait_recv()
        (inv_t,) = inverses([in_b[0] - out_a[0]])
        xj = nt(inv_t, keep[11])
        keep[0] = keep[0] - nn(keep[11], xj)
        send_b(1).wait_recv()
        xr = nn(inv_t, in_b[1] - out_a[1])
        keep[1] = keep[1] - nn(keep[11], xr)
        keep[13] = xj
        keep[14] = xr

        @pl.when(jnp.logical_not(is_middle))
        def _():
            out_b[0] = keep[0]
            send_b(0).start()
            out_b[1] = keep[1]
            send_b(1).start()

    @pl.when(takes_a)
    def _():
        send_a(0).wait_recv()
        send_a(1).wait_recv()
        keep[0] = keep[0] - in_a[0]
        keep[1] = keep[1] - in_a[1]

    @pl.when(is_left & jnp.logical_not(is_outer))
    def _():
        send_b(0).wait_recv()
        keep[0] = keep[0] - in_b[0]

    @pl.when(is_left | is_middle)
    def _():
        (inv_n,) = inverses([keep[0]])
        keep[15] = inv_n

    @pl.when(is_left & jnp.logical_not(is_outer))
    def _():
        send_b(1).wait_recv()
        keep[1] = keep[1] - in_b[1]

    @pl.when(is_middle & jnp.logical_not(is_left))
    def _():
        send_a(2).wait_recv()
        keep[12] = in_a[2]

    @pl.when(is_middle)
    def _():
        inv_n = keep[15]
        out_c[0] = nn(inv_n, keep[12])
        send_c(0).start()
        out_c[1] = nn(inv_n, keep[1])
        send_c(1).start()
        send_c(0).wait_recv()
        (inv_m,) = inverses([keep[0] - nn(keep[12], in_c[0])])
        send_c(1).wait_recv()
        x0 = nn(inv_m, keep[1] - nn(keep[12], in_c[1]))
        out_d[...] = x0

        @pl.when(is_left & jnp.logical_not(is_outer))
        def _():
            send_d().start()

        in_d[...] = in_c[1] - nn(in_c[0], x0)
        send_c(0).wait_send()
        send_c(1).wait_send()

    @pl.when(is_left & jnp.logical_not(is_middle))
    def _():
        inv_n = keep[15]
        xj = nn(inv_n, keep[12])
        out_b[0] = tn(keep[12], xj)
        send_b(0).start()
        xr = nn(inv_n, keep[1])
        out_b[1] = tn(keep[12], xr)
        send_b(1).start()
        send_d().wait_recv()
        out_d[...] = xr - nn(xj, in_d[...])

    @pl.when(is_left & jnp.logical_not(is_outer) & jnp.logical_not(is_middle))
    def _():
        send_d().start()

    @pl.when(is_left)
    def _():
        keep[0] = in_d[...]
        keep[1] = out_d[...]

    @pl.when(jnp.logical_not(is_left))
    def _():
        @pl.when(is_middle)
        def _():
            keep[1] = out_d[...]

        @pl.when(jnp.logical_not(is_middle))
        def _():
            send_d().wait_recv()
            keep[1] = in_d[...]

        @pl.when(is_outer)
        def _():
            keep[0] = jnp.zeros(shape, jnp.float32)

        @pl.when(jnp.logical_not(is_outer))
        def _():
            following = keep[14] - nn(keep[13], keep[1])
            keep[0] = following
            out_d[...] = following
            send_d().start()

    @pl.when(jnp.logical_not(is_middle))
    def _():
        send_b(0).wait_send()
        send_b(1).wait_send()

    x0, xt = keep[1], keep[0]
    xb = keep[10] - nn(keep[8], x0) - nn(keep[9], xt)
    xa = keep[3] - nn(keep[2], x0) - nn(keep[4], xb)
    xd = keep[7] - nn(keep[5], xt) - nn(keep[6], xb)
    blocks = [
        x0, jnp.where(three, xa, xb), jnp.where(three, xb, zero), jnp.where(four, xd, zero)
    ]
    for j in range(cap):
        for i in range(ne):
            out_e[i, j * rows : (j + 1) * rows, :] = blocks[j][i * rows : (i + 1) * rows, :]

    def send_e(i):
        to = lax.rem(e + i, ne)
        return pltpu.make_async_remote_copy(
            src_ref=out_e.at[to], dst_ref=in_e.at[e], send_sem=se.at[i], recv_sem=re.at[i],
            device_id=(to, p), device_id_type=MESH,
        )

    for i in range(1, ne):
        send_e(i).start()
    for j in range(cap):
        lesser[0, j] = blocks[j]
    in_e[e] = out_e[e]

    def weights_of(k, carry):
        here = energies[k].astype(jnp.float32)
        for f in range(ne):
            t = jnp.full((8, 128), energies[f].astype(jnp.float32) - here, jnp.float32)
            weights[k, f] = 0.5 * (
                1.6 * jnp.exp(-((t - 6.0) ** 2) / 18.0) + 0.6 * jnp.exp(-((t + 6.0) ** 2) / 18.0)
            )
        return carry

    lax.fori_loop(0, ne, weights_of, 0)
    for i in range(1, ne):
        send_e(i).wait_recv()

    def row_of(k, carry):
        terms = [weights[k, f][:1] * in_e[f] for f in range(ne)]
        while len(terms) > 1:
            pairs = [terms[i : i + 2] for i in range(0, len(terms), 2)]
            terms = [q[0] + q[1] if len(q) == 2 else q[0] for q in pairs]
        for j in range(cap):
            selfe[k, j] = terms[0][j * rows : (j + 1) * rows, :]
        return carry

    lax.fori_loop(0, ne, row_of, 0)
    for i in range(1, ne):
        send_e(i).wait_send()

    @pl.when(is_left)
    def _():
        send_a(0).wait_send()
        send_a(1).wait_send()

    @pl.when(p == half - 1)
    def _():
        send_a(2).wait_send()

    @pl.when(jnp.logical_not(is_outer))
    def _():
        send_d().wait_send()


def per_device(ne, nslab, counts, energies, ham, link, inj):
    cap, width, _ = ham.shape
    rows = width // ne
    block = lambda *n: pltpu.VMEM((*n, width, width), jnp.float32)
    dma = pltpu.SemaphoreType.DMA
    vmem = pl.BlockSpec(memory_space=pltpu.VMEM)
    hbm = pl.BlockSpec(memory_space=pltpu.HBM)
    exchange = pltpu.VMEM((ne, cap * rows, width), jnp.float32)
    return pl.pallas_call(
        functools.partial(kernel, ne, nslab),
        out_shape=(
            jax.ShapeDtypeStruct(inj.shape, jnp.float32),
            jax.ShapeDtypeStruct((ne, cap, rows, width), jnp.float32),
        ),
        in_specs=[hbm] * 5,
        out_specs=(vmem, vmem),
        scratch_shapes=[
            pltpu.SMEM(counts.shape, jnp.int32), pltpu.SMEM(energies.shape, jnp.int32),
            pltpu.VMEM(ham.shape, jnp.float32), pltpu.VMEM(link.shape, jnp.float32),
            pltpu.VMEM(inj.shape, jnp.float32), dma((5,)),
            block(16), block(3), block(3), block(2), block(2), block(2), block(2), block(), block(),
            exchange, exchange, pltpu.VMEM((ne, ne, 8, 128), jnp.float32),
            dma((3,)), dma((3,)), dma((2,)), dma((2,)), dma((2,)), dma((2,)), dma, dma,
            dma((ne,)), dma((ne,)),
        ],
        compiler_params=pltpu.CompilerParams(
            collective_id=0, has_side_effects=True, vmem_limit_bytes=62 << 20
        ),
    )(counts, energies, ham, link, inj)


def solution(mesh):
    return jax.shard_map(
        functools.partial(per_device, mesh.shape["energy"], mesh.shape["slab"]),
        mesh=mesh,
        in_specs=(
            P(),
            P(),
            P("slab", None, None),
            P("slab", None, None),
            P("energy", "slab", None, None),
        ),
        out_specs=(P("energy", "slab", None, None), P(None, "slab", "energy", None)),
        check_vma=False,
    )
```

profile of v0, /device:TPU:0, one launch (start us, length us, event | category | flops | bytes accessed | tf_op | source)
XLA Modules:
  0.0 51.9 jit_solution(10024116345719736970)
XLA Ops:
  0.6 48.8 %shard_map.68 = (f32[1,4,128,128]{3,2,1,0:T(8,128)}, f32[8,4,16,128]{3,2,1,0:T(8,128)}) custom-call(s32[4]{0:T(128)} %counts_in.1, s32[8]{0:T(128)} %energies_in.1, f32[4,128,128]{2,1,0:T(8,128)} %ham_in.1, f32[4,128,128]{2,1,0:T(8,128)} %link_in.1, f32[1,4,128,128]{3,2,1,0:T(8,128)} %inj_in.1), custom_call_target="tpu_custom_call" | custom-call | tf_op jit(solution)/shard_map/pallas_call | solution.py:454
  49.5 0.0 copy-start
  49.5 1.7 %copy.9 = f32[1,4,128,128]{3,2,1,0:T(8,128)} copy(f32[1,4,128,128]{3,2,1,0:T(8,128)} %get-tuple-element.4) | data formatting | bytes 524288
  51.2 0.0 copy-done
  51.2 0.7 %copy.10 = f32[8,4,16,128]{3,2,1,0:T(8,128)} copy(f32[8,4,16,128]{3,2,1,0:T(8,128)S(1)} %copy-done) | data formatting | bytes 524288
Async XLA Ops:
  49.5 1.7 %copy-start = (f32[8,4,16,128]{3,2,1,0:T(8,128)S(1)}, f32[8,4,16,128]{3,2,1,0:T(8,128)}, u32[]{:S(2)}) copy-start(f32[8,4,16,128]{3,2,1,0:T(8,128)} %get-tuple-element.5) | copy-start | bytes 786436
where the time goes:
time: 52 us; the launch traced here: 51.9 us
  Pallas kernels  48.8 us (94%)
  local copies, waits for them, and re-layouts  2.42 us (5%)
  between operations  0.65 us (1%)
    pallas_call x1, Pallas kernels, per_device(): pl.pallas_call(functools.partial(kernel, ne, nslab), out_shape=(jax.Shape...  48.8 us
    unnamed x4, local copies, waits for them, and re-layouts  2.42 us

commit v1 on v0

--- a/solution.py
+++ b/solution.py
@@ -28,92 +28,79 @@
     return contract(left, right, 1, 1)
 
 
-def weighted(weights, rows):
-    terms = [w * r for w, r in zip(weights, rows)]
+def spread(x, q):
+    return jnp.broadcast_to(x[q : q + 1, :], (8, 128))
+
+
+def across(x, k):
+    return jnp.take_along_axis(x, jnp.full((8, 128), k, jnp.int32), axis=1)
+
+
+def tree(terms):
     while len(terms) > 1:
         terms = [terms[i] + terms[i + 1] for i in range(0, len(terms), 2)]
     return terms[0]
 
 
-def small_inverse(block):
-    size = len(block)
-    if size == 2:
-        a, b, d = block[0][0], block[0][1], block[1][1]
-        scale = 1.0 / (a * d - b * b)
-        a, b, d = a * scale, b * scale, d * scale
-        return lambda rows: [d * rows[0] - b * rows[1], a * rows[1] - b * rows[0]]
-    h = size // 2
-    first = small_inverse([r[:h] for r in block[:h]])
-    columns = [[block[i][h + j] for i in range(h)] for j in range(h)]
-    cross = [first(column) for column in columns]
-    schur = [[None] * h for _ in range(h)]
-    for i in range(h):
-        for j in range(i, h):
-            schur[i][j] = schur[j][i] = block[h + i][h + j] - weighted(columns[i], cross[j])
-    second = small_inverse(schur)
-
-    def apply(rows):
-        upper = first(rows[:h])
-        x2 = second([rows[h + i] - weighted(cross[i], rows[:h]) for i in range(h)])
-        x1 = [upper[i] - weighted([cross[j][i] for j in range(h)], x2) for i in range(h)]
-        return x1 + x2
-
-    return apply
-
-
-def sweep(chunks, k, size):
+def pivot_rows(rows, columns, sub):
+    for q in range(0, 8, 2):
+        first, both = sub == q, (sub == q) | (sub == q + 1)
+        x, y = columns[q], columns[q + 1]
+        a, b, d = spread(x, q), spread(y, q), spread(y, q + 1)
+        inv = 1.0 / (a * d - b * b)
+        gx = jnp.where(both, jnp.where(first, -1.0, 0.0), x)
+        gy = jnp.where(both, jnp.where(first, 0.0, -1.0), y)
+        fx = d * gx - b * gy
+        fy = a * gy - b * gx
+        ex, ey = fx * inv, fy * inv
+        for j in range(q + 2, 8):
+            u, v = spread(columns[j], q), spread(columns[j], q + 1)
+            rest = jnp.where(both, 0.0, columns[j])
+            change = (fx * u + fy * v) * inv if j < q + 4 else ex * u + ey * v
+            columns[j] = rest - change
+        change = ex * spread(rows, q) + ey * spread(rows, q + 1)
+        rows = jnp.where(both, 0.0, rows) - change
+    return rows
+
+
+def sweep(chunks, at, k, lane, sub):
+    columns = [[across(c, k + q) for c in chunks] for q in range(8)]
+    inside = (lane >= k) & (lane < k + 8)
+    pivots = jnp.where(inside, jnp.where(lane - k == sub, -1.0, 0.0), chunks[at])
+    solved = pivot_rows(pivots, [column[at] for column in columns], sub)
+    rows = [spread(solved, q) for q in range(8)]
+    out = []
+    for c in range(len(chunks)):
+        if c == at:
+            out.append(solved)
+        else:
+            change = tree([columns[q][c] * rows[q] for q in range(8)])
+            out.append(jnp.where(inside, 0.0, chunks[c]) - change)
+    return out
+
+
+def inverses(matrices):
+    width = matrices[0].shape[0]
+    size = width // 2 if len(matrices) == 1 else width // 4
     lane = lax.broadcasted_iota(jnp.int32, (8, 128), 1)
     sub = lax.broadcasted_iota(jnp.int32, (8, 128), 0)
-    at, o = k // 8, k % 8
-    columns = [
-        [jnp.broadcast_to(c[:, k + q : k + q + 1], (8, 128)) for c in chunks] for q in range(size)
-    ]
-    block = [[None] * size for _ in range(size)]
-    for i in range(size):
-        for j in range(i, size):
-            block[i][j] = block[j][i] = columns[i][at][o + j : o + j + 1, :]
-    inside = (lane >= k) & (lane < k + size)
-    pivots = jnp.where(inside, jnp.where(lane - k == sub - o, -1.0, 0.0), chunks[at])
-    solved = small_inverse(block)([pivots[o + i : o + i + 1, :] for i in range(size)])
-    solved = [jnp.broadcast_to(x, (8, 128)) for x in solved]
-    out = []
-    for c in range(len(chunks)):
-        change = weighted([columns[q][c] for q in range(size)], solved)
-        value = jnp.where(inside, 0.0, chunks[c]) - change
-        if c == at:
-            for i in range(size):
-                value = jnp.where(sub == o + i, solved[i], value)
-        out.append(value)
-    return out
-
-
-def inverses(matrices):
-    size, unroll = (8, 2) if len(matrices) == 1 else (4, 4)
-    lane = lax.broadcasted_iota(jnp.int32, (8, 128), 1)
-    sub = lax.broadcasted_iota(jnp.int32, (8, 128), 0)
-    count = matrices[0].shape[0] // 8
-    scales, sets = [], []
-    for matrix in matrices:
-        chunks = [matrix[8 * i : 8 * i + 8, :] for i in range(count)]
-        top = jnp.zeros((8, 128), jnp.float32)
-        for i in range(count):
-            top = jnp.maximum(top, jnp.where(lane - sub == 8 * i, chunks[i], 0.0))
-        scale = 1.0 / jnp.max(top, axis=(0, 1), keepdims=True)
-        scales.append(scale)
-        sets.append([c * scale for c in chunks])
-
-    def body(_, carry):
-        sets = [list(s) for s in carry]
-        for k in range(0, 8 * unroll, size):
-            sets = [sweep(s, k, size) for s in sets]
-        return [
-            [pltpu.roll(c, 128 - 8 * unroll, 1) for c in s[unroll:] + s[:unroll]] for s in sets
-        ]
-
-    sets = lax.fori_loop(0, count // unroll, body, sets)
-    return [
-        jnp.concatenate([c * -scale for c in s], axis=0) for s, scale in zip(sets, scales)
-    ]
+    count = width // 8
+    sets = [[m[8 * i : 8 * i + 8, :] for i in range(count)] for m in matrices]
+    for start in range(0, width, size):
+        low, high = start // 8, (start + size) // 8
+        panels = [s[low:high] for s in sets]
+        for g in range(high - low):
+            panels = [sweep(p, g, start + 8 * g, lane, sub) for p in panels]
+        for i in range(len(sets)):
+            rest = jnp.concatenate(sets[i][:low] + sets[i][high:], axis=0)
+            zero = jnp.zeros((8, width), jnp.float32)
+            panel = jnp.concatenate([zero] * low + panels[i] + [zero] * (count - high), axis=0)
+            column = lax.broadcasted_iota(jnp.int32, rest.shape, 1)
+            inside = (column >= start) & (column < start + size)
+            rest = jnp.where(inside, 0.0, rest) - nn(rest, panel)
+            rest = [rest[8 * j : 8 * j + 8, :] for j in range(count - high + low)]
+            sets[i] = rest[:low] + panels[i] + rest[low:]
+    return [-jnp.concatenate(s, axis=0) for s in sets]
 
 
 def kernel(

time: 52 us -> 41.1 us (0.79)
  Pallas kernels: 48.8 us -> 37.9 us
    pallas_call x1, Pallas kernels: 48.8 us -> 37.9 us  [per_device(): pl.pallas_call(functools.partial(kernel, ne, nslab), out_shape=(jax.Shape...]
where the time goes in v1:
time: 41.1 us; the launch traced here: 41 us
  Pallas kernels  37.9 us (92%)
  local copies, waits for them, and re-layouts  2.42 us (6%)
  between operations  0.65 us (2%)
    pallas_call x1, Pallas kernels, per_device(): pl.pallas_call(functools.partial(kernel, ne, nslab), out_shape=(jax.Shape...  37.9 us
    unnamed x4, local copies, waits for them, and re-layouts  2.42 us

profile of v1, /device:TPU:0, one launch (start us, length us, event | category | flops | bytes accessed | tf_op | source)
XLA Modules:
  0.0 41.0 jit_solution(10376968165328093717)
XLA Ops:
  0.6 37.9 %shard_map.68 = (f32[1,4,128,128]{3,2,1,0:T(8,128)}, f32[8,4,16,128]{3,2,1,0:T(8,128)}) custom-call(s32[4]{0:T(128)} %counts_in.1, s32[8]{0:T(128)} %energies_in.1, f32[4,128,128]{2,1,0:T(8,128)} %ham_in.1, f32[4,128,128]{2,1,0:T(8,128)} %link_in.1, f32[1,4,128,128]{3,2,1,0:T(8,128)} %inj_in.1), custom_call_target="tpu_custom_call" | custom-call | tf_op jit(solution)/shard_map/pallas_call | solution.py:441
  38.6 0.0 copy-start
  38.6 1.7 %copy.9 = f32[1,4,128,128]{3,2,1,0:T(8,128)} copy(f32[1,4,128,128]{3,2,1,0:T(8,128)} %get-tuple-element.4) | data formatting | bytes 524288
  40.3 0.0 copy-done
  40.3 0.7 %copy.10 = f32[8,4,16,128]{3,2,1,0:T(8,128)} copy(f32[8,4,16,128]{3,2,1,0:T(8,128)S(1)} %copy-done) | data formatting | bytes 524288
Async XLA Ops:
  38.6 1.7 %copy-start = (f32[8,4,16,128]{3,2,1,0:T(8,128)S(1)}, f32[8,4,16,128]{3,2,1,0:T(8,128)}, u32[]{:S(2)}) copy-start(f32[8,4,16,128]{3,2,1,0:T(8,128)} %get-tuple-element.5) | copy-start | bytes 786436

commit v2 on v1

--- a/solution.py
+++ b/solution.py
@@ -430,6 +430,325 @@
         send_d().wait_send()
 
 
+def short_kernel(
+    ne, nslab, counts_in, energies_in, ham_in, link_in, inj_in, lesser, selfe,
+    counts, energies, ham, link, inj, si,
+    keep, here, there, out_e, in_e, weights, ss, rs, se, re,
+):
+    pairs = [
+        (counts_in, counts), (energies_in, energies), (ham_in, ham), (link_in, link), (inj_in, inj)
+    ]
+    staged = [pltpu.make_async_copy(a, b, si.at[i]) for i, (a, b) in enumerate(pairs)]
+    for copy in staged:
+        copy.start()
+    e = lax.axis_index("energy")
+    p = lax.axis_index("slab")
+    width = ham.shape[1]
+    cap = ham.shape[0]
+    rows = width // ne
+    last = nslab - 1
+    is_outer = (p == 0) | (p == last)
+    is_left = p < 2
+    near = jnp.where(is_left, 1 - p, 5 - p)
+    middle = jnp.where(is_left, 2, 1)
+    far = last - p
+
+    barrier = pltpu.get_barrier_semaphore()
+    for i in range(1, ne):
+        pl.semaphore_signal(
+            barrier, inc=1, device_id=(lax.rem(e + i, ne), p), device_id_type=MESH
+        )
+    for i in range(1, nslab):
+        pl.semaphore_signal(
+            barrier, inc=1, device_id=(e, lax.rem(p + i, nslab)), device_id_type=MESH
+        )
+
+    C, N, K, R, A0, A1, S0, S1, X, Y, D0, D1 = range(12)
+
+    def send(what, slot, to):
+        return pltpu.make_async_remote_copy(
+            src_ref=here.at[what], dst_ref=there.at[what],
+            send_sem=ss.at[slot], recv_sem=rs.at[what],
+            device_id=(e, to), device_id_type=MESH,
+        )
+
+    def arrived(what):
+        send(what, what, near).wait_recv()
+
+    def from_inner():
+        return [send(N, N, near), send(K, K, near), send(R, R, near)]
+
+    def from_second():
+        return [send(A0, A0, 2), send(A1, A1, 2)]
+
+    def from_third(i):
+        return [send(S0 + i, 12 + 3 * i + j, to) for j, to in enumerate((0, 1, last))]
+
+    def from_outer(i):
+        return [
+            send(D0 + i, 18 + 2 * i, far), send(D0 + i, 19 + 2 * i, middle), send(X + i, X + i, near)
+        ]
+
+    for copy in staged:
+        copy.wait()
+    shape = (width, width)
+    eye = (
+        lax.broadcasted_iota(jnp.int32, shape, 0) == lax.broadcasted_iota(jnp.int32, shape, 1)
+    ).astype(jnp.float32)
+    shift = 0.02 + 0.06 * energies[e].astype(jnp.float32) / (4 * ne)
+    shifted = eye * shift
+    at = jnp.full(shape, p, jnp.int32)
+    third, inner = at == 2, at < last
+    count = jnp.full(shape, counts[p], jnp.int32) - third.astype(jnp.int32)
+    one, two, three, four = count == 1, count == 2, count >= 3, count == 4
+    zero = jnp.zeros(shape, jnp.float32)
+
+    def ending(blocks):
+        return jnp.where(one, blocks[1], jnp.where(two, blocks[2], blocks[3]))
+
+    here[C] = ending(link).T
+    diag_a = jnp.where(three, ham[1] + shifted, eye)
+    diag_d = jnp.where(four, ham[3] + shifted, eye)
+    inv_a, inv_d = inverses([diag_a, diag_d])
+    link_0a = jnp.where(three, link[0], zero)
+    link_0b = jnp.where(two, link[0], zero)
+    link_0t = jnp.where(one, link[0], zero)
+    link_ab = jnp.where(three, link[1], zero)
+    link_bd = jnp.where(four, link[2], zero)
+    link_dt = jnp.where(four & inner, link[3], zero)
+    link_bt = jnp.where(two & inner, link[1], jnp.where((count == 3) & inner, link[2], zero))
+    rhs_a = jnp.where(three, inj[0, 1], zero)
+    rhs_b = jnp.where(three, inj[0, 2], jnp.where(two, inj[0, 1], zero))
+    rhs_d = jnp.where(four, inj[0, 3], zero)
+    diag_b = jnp.where(three, ham[2] + shifted, jnp.where(two, ham[1] + shifted, eye))
+
+    xab = nn(inv_a, link_ab)
+    xdb = nt(inv_d, link_bd)
+    diag_b = diag_b - tn(link_ab, xab) - nn(link_bd, xdb)
+    keep[2] = inv_a
+    keep[3] = inv_d
+    keep[4] = xab
+    keep[6] = xdb
+    pl.semaphore_wait(barrier, ne + nslab - 2)
+
+    @pl.when(p == 2)
+    def _():
+        send(C, C, last).start()
+
+    inv_a, inv_d, xab, xdb = keep[2], keep[3], keep[4], keep[6]
+    (inv_b,) = inverses([diag_b])
+    link_0b = link_0b - nn(link_0a, xab)
+    xa0 = nt(inv_a, link_0a)
+    xdt = nn(inv_d, link_dt)
+    link_bt = link_bt - nn(link_bd, xdt)
+    xb0 = nt(inv_b, link_0b)
+    xbt = nn(inv_b, link_bt)
+    node = ham[0] + shifted - nn(link_0a, xa0) - nn(link_0b, xb0)
+    ahead = tn(link_dt, xdt) + tn(link_bt, xbt)
+    keep[0] = node
+    here[A0] = ahead
+    here[N] = jnp.where(third, ending(ham) + shifted - ahead, node)
+
+    @pl.when(jnp.logical_not(is_outer))
+    def _():
+        from_inner()[0].start()
+
+    @pl.when(p == 1)
+    def _():
+        from_second()[0].start()
+
+    own_link = link_0t - nn(link_0b, xbt)
+    here[K] = jnp.where(third, own_link.T, own_link)
+    keep[2] = xa0
+    keep[5] = xdt
+    keep[8] = xb0
+    keep[9] = xbt
+
+    @pl.when(jnp.logical_not(is_outer))
+    def _():
+        from_inner()[1].start()
+
+    xaf = nn(inv_a, rhs_a)
+    xdf = nn(inv_d, rhs_d)
+    rhs_b = rhs_b - tn(link_ab, xaf) - nn(link_bd, xdf)
+    xbf = nn(inv_b, rhs_b)
+    node_rhs = inj[0, 0] - nn(link_0a, xaf) - nn(link_0b, xbf)
+    ahead = tn(link_dt, xdf) + tn(link_bt, xbf)
+    keep[1] = node_rhs
+    here[A1] = ahead
+    here[R] = jnp.where(third, ending(inj.at[0]) - ahead, node_rhs)
+    keep[3], keep[7], keep[10] = xaf, xdf, xbf
+
+    @pl.when(jnp.logical_not(is_outer))
+    def _():
+        from_inner()[2].start()
+
+    @pl.when(p == 1)
+    def _():
+        from_second()[1].start()
+
+    @pl.when(p == 2)
+    def _():
+        arrived(A0)
+        here[S0] = keep[0] - there[A0]
+        for copy in from_third(0):
+            copy.start()
+        arrived(A1)
+        here[S1] = keep[1] - there[A1]
+        for copy in from_third(1):
+            copy.start()
+
+    @pl.when(is_outer)
+    def _():
+        (inv_n,) = inverses([keep[0]])
+        keep[15] = inv_n
+
+        @pl.when(p == 0)
+        def _():
+            keep[11] = here[K]
+
+        @pl.when(p == last)
+        def _():
+            arrived(C)
+            keep[11] = there[C]
+
+        xj = nn(keep[15], keep[11])
+        keep[12] = xj
+        arrived(N)
+        (inv_m,) = inverses([there[N] - here[A0] - tn(keep[11], xj)])
+        keep[14] = inv_m
+        xr = nn(keep[15], keep[1])
+        keep[13] = xr
+        below = here[A1] + tn(keep[11], xr)
+        arrived(K)
+        x = nn(inv_m, there[K])
+        here[X] = x
+        here[D0] = tn(there[K], x)
+        for copy in from_outer(0):
+            copy.start()
+        arrived(R)
+        y = nn(keep[14], there[R] - below)
+        here[Y] = y
+        here[D1] = tn(there[K], y)
+        for copy in from_outer(1):
+            copy.start()
+
+    @pl.when(jnp.logical_not(is_outer))
+    def _():
+        arrived(X)
+        x = there[X]
+        here[X] = x
+        here[D0] = tn(here[K], x)
+
+    @pl.when(p != 2)
+    def _():
+        arrived(S0)
+        here[S0] = there[S0]
+
+    arrived(D0)
+    (inv_s,) = inverses([here[S0] - here[D0] - there[D0]])
+    keep[15] = inv_s
+
+    @pl.when(jnp.logical_not(is_outer))
+    def _():
+        arrived(Y)
+        y = there[Y]
+        here[Y] = y
+        here[D1] = tn(here[K], y)
+
+    @pl.when(p != 2)
+    def _():
+        arrived(S1)
+        here[S1] = there[S1]
+
+    arrived(D1)
+    x2 = nn(keep[15], here[S1] - here[D1] - there[D1])
+    end = here[Y] - nn(here[X], x2)
+
+    @pl.when(is_outer)
+    def _():
+        keep[0] = end
+        keep[1] = keep[13] - nn(keep[12], end)
+
+    @pl.when(jnp.logical_not(is_outer))
+    def _():
+        keep[0] = jnp.where(third, end, x2)
+        keep[1] = jnp.where(third, x2, end)
+
+    x0, xt = keep[1], keep[0]
+    xb = keep[10] - nn(keep[8], x0) - nn(keep[9], xt)
+    xa = keep[3] - nn(keep[2], x0) - nn(keep[4], xb)
+    xd = keep[7] - nn(keep[5], xt) - nn(keep[6], xb)
+    blocks = [
+        x0,
+        jnp.where(three, xa, jnp.where(one, xt, xb)),
+        jnp.where(three, xb, jnp.where(two & third, xt, zero)),
+        jnp.where(four, xd, jnp.where(three & third, xt, zero)),
+    ]
+    for j in range(cap):
+        for i in range(ne):
+            out_e[i, j * rows : (j + 1) * rows, :] = blocks[j][i * rows : (i + 1) * rows, :]
+
+    def send_e(i):
+        to = lax.rem(e + i, ne)
+        return pltpu.make_async_remote_copy(
+            src_ref=out_e.at[to], dst_ref=in_e.at[e], send_sem=se.at[i], recv_sem=re.at[i],
+            device_id=(to, p), device_id_type=MESH,
+        )
+
+    for i in range(1, ne):
+        send_e(i).start()
+    for j in range(cap):
+        lesser[0, j] = blocks[j]
+    in_e[e] = out_e[e]
+
+    def weights_of(k, carry):
+        here = energies[k].astype(jnp.float32)
+        for f in range(ne):
+            t = jnp.full((8, 128), energies[f].astype(jnp.float32) - here, jnp.float32)
+            weights[k, f] = 0.5 * (
+                1.6 * jnp.exp(-((t - 6.0) ** 2) / 18.0) + 0.6 * jnp.exp(-((t + 6.0) ** 2) / 18.0)
+            )
+        return carry
+
+    lax.fori_loop(0, ne, weights_of, 0)
+    for i in range(1, ne):
+        send_e(i).wait_recv()
+
+    def row_of(k, carry):
+        terms = [weights[k, f][:1] * in_e[f] for f in range(ne)]
+        while len(terms) > 1:
+            pairs = [terms[i : i + 2] for i in range(0, len(terms), 2)]
+            terms = [q[0] + q[1] if len(q) == 2 else q[0] for q in pairs]
+        for j in range(cap):
+            selfe[k, j] = terms[0][j * rows : (j + 1) * rows, :]
+        return carry
+
+    lax.fori_loop(0, ne, row_of, 0)
+    for i in range(1, ne):
+        send_e(i).wait_send()
+
+    @pl.when(jnp.logical_not(is_outer))
+    def _():
+        for copy in from_inner():
+            copy.wait_send()
+
+    @pl.when(is_outer)
+    def _():
+        for copy in from_outer(0) + from_outer(1):
+            copy.wait_send()
+
+    @pl.when(p == 1)
+    def _():
+        for copy in from_second():
+            copy.wait_send()
+
+    @pl.when(p == 2)
+    def _():
+        for copy in [send(C, C, last)] + from_third(0) + from_third(1):
+            copy.wait_send()
+
+
 def per_device(ne, nslab, counts, energies, ham, link, inj):
     cap, width, _ = ham.shape
     rows = width // ne
@@ -438,23 +757,30 @@
     vmem = pl.BlockSpec(memory_space=pltpu.VMEM)
     hbm = pl.BlockSpec(memory_space=pltpu.HBM)
     exchange = pltpu.VMEM((ne, cap * rows, width), jnp.float32)
+    staging = [
+        pltpu.SMEM(counts.shape, jnp.int32), pltpu.SMEM(energies.shape, jnp.int32),
+        pltpu.VMEM(ham.shape, jnp.float32), pltpu.VMEM(link.shape, jnp.float32),
+        pltpu.VMEM(inj.shape, jnp.float32), dma((5,)),
+    ]
+    last = [exchange, exchange, pltpu.VMEM((ne, ne, 8, 128), jnp.float32)]
+    if nslab == 4:
+        body = short_kernel
+        scratch = [block(16), block(12), block(12), *last, dma((22,)), dma((12,))]
+    else:
+        body = kernel
+        scratch = [
+            block(16), block(3), block(3), block(2), block(2), block(2), block(2), block(), block(),
+            *last, dma((3,)), dma((3,)), dma((2,)), dma((2,)), dma((2,)), dma((2,)), dma, dma,
+        ]
     return pl.pallas_call(
-        functools.partial(kernel, ne, nslab),
+        functools.partial(body, ne, nslab),
         out_shape=(
             jax.ShapeDtypeStruct(inj.shape, jnp.float32),
             jax.ShapeDtypeStruct((ne, cap, rows, width), jnp.float32),
         ),
         in_specs=[hbm] * 5,
         out_specs=(vmem, vmem),
-        scratch_shapes=[
-            pltpu.SMEM(counts.shape, jnp.int32), pltpu.SMEM(energies.shape, jnp.int32),
-            pltpu.VMEM(ham.shape, jnp.float32), pltpu.VMEM(link.shape, jnp.float32),
-            pltpu.VMEM(inj.shape, jnp.float32), dma((5,)),
-            block(16), block(3), block(3), block(2), block(2), block(2), block(2), block(), block(),
-            exchange, exchange, pltpu.VMEM((ne, ne, 8, 128), jnp.float32),
-            dma((3,)), dma((3,)), dma((2,)), dma((2,)), dma((2,)), dma((2,)), dma, dma,
-            dma((ne,)), dma((ne,)),
-        ],
+        scratch_shapes=[*staging, *scratch, dma((ne,)), dma((ne,))],
         compiler_params=pltpu.CompilerParams(
             collective_id=0, has_side_effects=True, vmem_limit_bytes=62 << 20
         ),

time: 41.1 us -> 39 us (0.949)
  Pallas kernels: 37.9 us -> 35.8 us
    pallas_call x1, Pallas kernels: 37.9 us -> 35.8 us  [per_device(): pl.pallas_call(functools.partial(body, ne, nslab), out_shape=(jax.ShapeDt...]
where the time goes in v2:
time: 39 us; the launch traced here: 38.8 us
  Pallas kernels  35.8 us (92%)
  local copies, waits for them, and re-layouts  2.42 us (6%)
  between operations  0.65 us (2%)
    pallas_call x1, Pallas kernels, per_device(): pl.pallas_call(functools.partial(body, ne, nslab), out_shape=(jax.ShapeDt...  35.8 us
    unnamed x4, local copies, waits for them, and re-layouts  2.42 us

profile of v2, /device:TPU:0, one launch (start us, length us, event | category | flops | bytes accessed | tf_op | source)
XLA Modules:
  0.0 38.8 jit_solution(1504710647550855717)
XLA Ops:
  0.6 35.8 %shard_map.68 = (f32[1,4,128,128]{3,2,1,0:T(8,128)}, f32[8,4,16,128]{3,2,1,0:T(8,128)}) custom-call(s32[4]{0:T(128)} %counts_in.1, s32[8]{0:T(128)} %energies_in.1, f32[4,128,128]{2,1,0:T(8,128)} %ham_in.1, f32[4,128,128]{2,1,0:T(8,128)} %link_in.1, f32[1,4,128,128]{3,2,1,0:T(8,128)} %inj_in.1), custom_call_target="tpu_custom_call" | custom-call | tf_op jit(solution)/shard_map/pallas_call | solution.py:775
  36.4 0.0 copy-start
  36.4 1.7 %copy.9 = f32[1,4,128,128]{3,2,1,0:T(8,128)} copy(f32[1,4,128,128]{3,2,1,0:T(8,128)} %get-tuple-element.4) | data formatting | bytes 524288
  38.1 0.0 copy-done
  38.1 0.7 %copy.10 = f32[8,4,16,128]{3,2,1,0:T(8,128)} copy(f32[8,4,16,128]{3,2,1,0:T(8,128)S(1)} %copy-done) | data formatting | bytes 524288
Async XLA Ops:
  36.4 1.7 %copy-start = (f32[8,4,16,128]{3,2,1,0:T(8,128)S(1)}, f32[8,4,16,128]{3,2,1,0:T(8,128)}, u32[]{:S(2)}) copy-start(f32[8,4,16,128]{3,2,1,0:T(8,128)} %get-tuple-element.5) | copy-start | bytes 786436

commit v3 on v2

--- a/solution.py
+++ b/solution.py
@@ -433,7 +433,7 @@
 def short_kernel(
     ne, nslab, counts_in, energies_in, ham_in, link_in, inj_in, lesser, selfe,
     counts, energies, ham, link, inj, si,
-    keep, here, there, out_e, in_e, weights, ss, rs, se, re,
+    keep, back, here, there, out_e, in_e, weights, ss, rs, se, re,
 ):
     pairs = [
         (counts_in, counts), (energies_in, energies), (ham_in, ham), (link_in, link), (inj_in, inj)
@@ -489,7 +489,7 @@
             send(D0 + i, 18 + 2 * i, far), send(D0 + i, 19 + 2 * i, middle), send(X + i, X + i, near)
         ]
 
-    for copy in staged:
+    for copy in staged[:3]:
         copy.wait()
     shape = (width, width)
     eye = (
@@ -506,10 +506,12 @@
     def ending(blocks):
         return jnp.where(one, blocks[1], jnp.where(two, blocks[2], blocks[3]))
 
-    here[C] = ending(link).T
     diag_a = jnp.where(three, ham[1] + shifted, eye)
     diag_d = jnp.where(four, ham[3] + shifted, eye)
     inv_a, inv_d = inverses([diag_a, diag_d])
+    for copy in staged[3:]:
+        copy.wait()
+    here[C] = ending(link).T
     link_0a = jnp.where(three, link[0], zero)
     link_0b = jnp.where(two, link[0], zero)
     link_0t = jnp.where(one, link[0], zero)
@@ -536,6 +538,9 @@
         send(C, C, last).start()
 
     inv_a, inv_d, xab, xdb = keep[2], keep[3], keep[4], keep[6]
+    xaf = nn(inv_a, rhs_a)
+    xdf = nn(inv_d, rhs_d)
+    rhs_b = rhs_b - tn(link_ab, xaf) - nn(link_bd, xdf)
     (inv_b,) = inverses([diag_b])
     link_0b = link_0b - nn(link_0a, xab)
     xa0 = nt(inv_a, link_0a)
@@ -563,24 +568,29 @@
     keep[5] = xdt
     keep[8] = xb0
     keep[9] = xbt
+    keep[3], keep[7], keep[10] = xaf, xdf, rhs_b
+    keep[11] = inv_b
+    keep[12] = link_0b
+    keep[13] = inj[0, 0] - nn(link_0a, xaf)
+    keep[14] = tn(link_dt, xdf)
+    keep[15] = link_bt
+
+    def right_sides():
+        xbf = nn(keep[11], keep[10])
+        node_rhs = keep[13] - nn(keep[12], xbf)
+        ahead = keep[14] + tn(keep[15], xbf)
+        keep[1] = node_rhs
+        keep[10] = xbf
+        here[A1] = ahead
+        here[R] = jnp.where(third, ending(inj.at[0]) - ahead, node_rhs)
 
     @pl.when(jnp.logical_not(is_outer))
     def _():
         from_inner()[1].start()
 
-    xaf = nn(inv_a, rhs_a)
-    xdf = nn(inv_d, rhs_d)
-    rhs_b = rhs_b - tn(link_ab, xaf) - nn(link_bd, xdf)
-    xbf = nn(inv_b, rhs_b)
-    node_rhs = inj[0, 0] - nn(link_0a, xaf) - nn(link_0b, xbf)
-    ahead = tn(link_dt, xdf) + tn(link_bt, xbf)
-    keep[1] = node_rhs
-    here[A1] = ahead
-    here[R] = jnp.where(third, ending(inj.at[0]) - ahead, node_rhs)
-    keep[3], keep[7], keep[10] = xaf, xdf, xbf
-
     @pl.when(jnp.logical_not(is_outer))
     def _():
+        right_sides()
         from_inner()[2].start()
 
     @pl.when(p == 1)
@@ -601,6 +611,7 @@
     @pl.when(is_outer)
     def _():
         (inv_n,) = inverses([keep[0]])
+        right_sides()
         keep[15] = inv_n
 
         @pl.when(p == 0)
@@ -632,6 +643,10 @@
         here[D1] = tn(there[K], y)
         for copy in from_outer(1):
             copy.start()
+        keep[0] = keep[13] - nn(keep[12], y)
+        keep[1] = y
+        keep[11] = -nn(keep[12], here[X])
+        keep[14] = here[X]
 
     @pl.when(jnp.logical_not(is_outer))
     def _():
@@ -639,6 +654,8 @@
         x = there[X]
         here[X] = x
         here[D0] = tn(here[K], x)
+        keep[11] = jnp.where(third, -eye, x)
+        keep[14] = jnp.where(third, x, -eye)
 
     @pl.when(p != 2)
     def _():
@@ -648,13 +665,20 @@
     arrived(D0)
     (inv_s,) = inverses([here[S0] - here[D0] - there[D0]])
     keep[15] = inv_s
+    g0, gt = keep[11], keep[14]
+    gb = -nn(keep[8], g0) - nn(keep[9], gt)
+    keep[12] = gb
+    keep[13] = -nn(keep[2], g0) - nn(keep[4], gb)
+    keep[11] = -nn(keep[5], gt) - nn(keep[6], gb)
+    back[0] = g0
 
     @pl.when(jnp.logical_not(is_outer))
     def _():
         arrived(Y)
         y = there[Y]
-        here[Y] = y
         here[D1] = tn(here[K], y)
+        keep[0] = jnp.where(third, zero, y)
+        keep[1] = jnp.where(third, y, zero)
 
     @pl.when(p != 2)
     def _():
@@ -663,22 +687,15 @@
 
     arrived(D1)
     x2 = nn(keep[15], here[S1] - here[D1] - there[D1])
-    end = here[Y] - nn(here[X], x2)
-
-    @pl.when(is_outer)
-    def _():
-        keep[0] = end
-        keep[1] = keep[13] - nn(keep[12], end)
-
-    @pl.when(jnp.logical_not(is_outer))
-    def _():
-        keep[0] = jnp.where(third, end, x2)
-        keep[1] = jnp.where(third, x2, end)
-
-    x0, xt = keep[1], keep[0]
-    xb = keep[10] - nn(keep[8], x0) - nn(keep[9], xt)
-    xa = keep[3] - nn(keep[2], x0) - nn(keep[4], xb)
-    xd = keep[7] - nn(keep[5], xt) - nn(keep[6], xb)
+    f0, ft = keep[0], keep[1]
+    fb = keep[10] - nn(keep[8], f0) - nn(keep[9], ft)
+    fa = keep[3] - nn(keep[2], f0) - nn(keep[4], fb)
+    fd = keep[7] - nn(keep[5], ft) - nn(keep[6], fb)
+    x0 = f0 - nn(back[0], x2)
+    xt = ft - nn(keep[14], x2)
+    xb = fb - nn(keep[12], x2)
+    xa = fa - nn(keep[13], x2)
+    xd = fd - nn(keep[11], x2)
     blocks = [
         x0,
         jnp.where(three, xa, jnp.where(one, xt, xb)),
@@ -747,6 +764,20 @@
     def _():
         for copy in [send(C, C, last)] + from_third(0) + from_third(1):
             copy.wait_send()
+
+
+def hand_over(*arrays):
+    def move(*refs):
+        for source, result in zip(refs, refs[len(arrays) :]):
+            result[...] = source[...]
+
+    vmem = pl.BlockSpec(memory_space=pltpu.VMEM)
+    return pl.pallas_call(
+        move,
+        out_shape=tuple(jax.ShapeDtypeStruct(a.shape, a.dtype) for a in arrays),
+        in_specs=[vmem] * len(arrays),
+        out_specs=(vmem,) * len(arrays),
+    )(*arrays)
 
 
 def per_device(ne, nslab, counts, energies, ham, link, inj):
@@ -765,14 +796,14 @@
     last = [exchange, exchange, pltpu.VMEM((ne, ne, 8, 128), jnp.float32)]
     if nslab == 4:
         body = short_kernel
-        scratch = [block(16), block(12), block(12), *last, dma((22,)), dma((12,))]
+        scratch = [block(16), block(1), block(12), block(12), *last, dma((22,)), dma((12,))]
     else:
         body = kernel
         scratch = [
             block(16), block(3), block(3), block(2), block(2), block(2), block(2), block(), block(),
             *last, dma((3,)), dma((3,)), dma((2,)), dma((2,)), dma((2,)), dma((2,)), dma, dma,
         ]
-    return pl.pallas_call(
+    results = pl.pallas_call(
         functools.partial(body, ne, nslab),
         out_shape=(
             jax.ShapeDtypeStruct(inj.shape, jnp.float32),
@@ -785,6 +816,7 @@
             collective_id=0, has_side_effects=True, vmem_limit_bytes=62 << 20
         ),
     )(counts, energies, ham, link, inj)
+    return hand_over(*results)
 
 
 def solution(mesh):

time: 39 us -> 36.9 us (0.946)
  local copies, waits for them, and re-layouts: 2.42 us -> 0 us
    unnamed x4 -> x0, local copies, waits for them, and re-layouts: 2.42 us -> none
    pallas_call x0 -> x1, Pallas kernels: none -> 1.84 us  [hand_over(): pl.pallas_call(move, out_shape=tuple((jax.ShapeDtypeStruct(a.shape, a.dty...]
    pallas_call x1, Pallas kernels: 35.8 us -> 34.3 us  [per_device(): pl.pallas_call(functools.partial(body, ne, nslab), out_shape=(jax.ShapeDt...]
where the time goes in v3:
time: 36.9 us; the launch traced here: 36.7 us
  Pallas kernels  36.1 us (98%)
  between operations  0.64 us (2%)
    pallas_call x1, Pallas kernels, per_device(): pl.pallas_call(functools.partial(body, ne, nslab), out_shape=(jax.ShapeDt...  34.3 us
    pallas_call x1, Pallas kernels, hand_over(): pl.pallas_call(move, out_shape=tuple((jax.ShapeDtypeStruct(a.shape, a.dty...  1.84 us

profile of v3, /device:TPU:0, one launch (start us, length us, event | category | flops | bytes accessed | tf_op | source)
XLA Modules:
  0.0 36.7 jit_solution(5087919081492327054)
XLA Ops:
  0.6 34.3 %shard_map.68 = (f32[1,4,128,128]{3,2,1,0:T(8,128)}, f32[8,4,16,128]{3,2,1,0:T(8,128)}) custom-call(s32[4]{0:T(128)} %counts_in.1, s32[8]{0:T(128)} %energies_in.1, f32[4,128,128]{2,1,0:T(8,128)} %ham_in.1, f32[4,128,128]{2,1,0:T(8,128)} %link_in.1, f32[1,4,128,128]{3,2,1,0:T(8,128)} %inj_in.1), custom_call_target="tpu_custom_call" | custom-call | tf_op jit(solution)/shard_map/pallas_call | solution.py:806
  34.9 1.8 %shard_map.69 = (f32[1,4,128,128]{3,2,1,0:T(8,128)}, f32[8,4,16,128]{3,2,1,0:T(8,128)}) custom-call(f32[1,4,128,128]{3,2,1,0:T(8,128)} %get-tuple-element.4.refs_0_, f32[8,4,16,128]{3,2,1,0:T(8,128)} %get-tuple-element.5.refs_1_), custom_call_target="tpu_custom_call" | custom-call | tf_op jit(solution)/shard_map/pallas_call | solution.py:775

commit v4 on v3

--- a/solution.py
+++ b/solution.py
@@ -430,6 +430,30 @@
         send_d().wait_send()
 
 
+def halves(x):
+    high = x.astype(jnp.bfloat16)
+    return high, (x - high.astype(jnp.float32)).astype(jnp.bfloat16)
+
+
+def product(left, right, a, b):
+    dims = (((a,), (b,)), ((), ()))
+    dot = lambda x, y: lax.dot_general(x, y, dims, preferred_element_type=jnp.float32)
+    (lh, ll), (rh, rl) = halves(left), halves(right)
+    return dot(lh, rh) + (dot(lh, rl) + dot(ll, rh))
+
+
+def nn3(left, right):
+    return product(left, right, 1, 0)
+
+
+def tn3(left, right):
+    return product(left, right, 0, 0)
+
+
+def nt3(left, right):
+    return product(left, right, 1, 1)
+
+
 def short_kernel(
     ne, nslab, counts_in, energies_in, ham_in, link_in, inj_in, lesser, selfe,
     counts, energies, ham, link, inj, si,
@@ -666,10 +690,10 @@
     (inv_s,) = inverses([here[S0] - here[D0] - there[D0]])
     keep[15] = inv_s
     g0, gt = keep[11], keep[14]
-    gb = -nn(keep[8], g0) - nn(keep[9], gt)
+    gb = -nn3(keep[8], g0) - nn3(keep[9], gt)
     keep[12] = gb
-    keep[13] = -nn(keep[2], g0) - nn(keep[4], gb)
-    keep[11] = -nn(keep[5], gt) - nn(keep[6], gb)
+    keep[13] = -nn3(keep[2], g0) - nn3(keep[4], gb)
+    keep[11] = -nn3(keep[5], gt) - nn3(keep[6], gb)
     back[0] = g0
 
     @pl.when(jnp.logical_not(is_outer))
@@ -688,14 +712,14 @@
     arrived(D1)
     x2 = nn(keep[15], here[S1] - here[D1] - there[D1])
     f0, ft = keep[0], keep[1]
-    fb = keep[10] - nn(keep[8], f0) - nn(keep[9], ft)
-    fa = keep[3] - nn(keep[2], f0) - nn(keep[4], fb)
-    fd = keep[7] - nn(keep[5], ft) - nn(keep[6], fb)
-    x0 = f0 - nn(back[0], x2)
-    xt = ft - nn(keep[14], x2)
-    xb = fb - nn(keep[12], x2)
-    xa = fa - nn(keep[13], x2)
-    xd = fd - nn(keep[11], x2)
+    fb = keep[10] - nn3(keep[8], f0) - nn3(keep[9], ft)
+    fa = keep[3] - nn3(keep[2], f0) - nn3(keep[4], fb)
+    fd = keep[7] - nn3(keep[5], ft) - nn3(keep[6], fb)
+    x0 = f0 - nn3(back[0], x2)
+    xt = ft - nn3(keep[14], x2)
+    xb = fb - nn3(keep[12], x2)
+    xa = fa - nn3(keep[13], x2)
+    xd = fd - nn3(keep[11], x2)
     blocks = [
         x0,
         jnp.where(three, xa, jnp.where(one, xt, xb)),

time: 36.9 us -> 36.6 us (level)
  no operation moved by 1% of the time
where the time goes in v4:
time: 36.6 us; the launch traced here: 36.5 us
  Pallas kernels  35.8 us (98%)
  between operations  0.64 us (2%)
    pallas_call x1, Pallas kernels, per_device(): pl.pallas_call(functools.partial(body, ne, nslab), out_shape=(jax.ShapeDt...  34 us
    pallas_call x1, Pallas kernels, hand_over(): pl.pallas_call(move, out_shape=tuple((jax.ShapeDtypeStruct(a.shape, a.dty...  1.84 us

profile of v4, /device:TPU:0, one launch (start us, length us, event | category | flops | bytes accessed | tf_op | source)
XLA Modules:
  0.0 36.5 jit_solution(1616947684944241350)
XLA Ops:
  0.6 34.0 %shard_map.68 = (f32[1,4,128,128]{3,2,1,0:T(8,128)}, f32[8,4,16,128]{3,2,1,0:T(8,128)}) custom-call(s32[4]{0:T(128)} %counts_in.1, s32[8]{0:T(128)} %energies_in.1, f32[4,128,128]{2,1,0:T(8,128)} %ham_in.1, f32[4,128,128]{2,1,0:T(8,128)} %link_in.1, f32[1,4,128,128]{3,2,1,0:T(8,128)} %inj_in.1), custom_call_target="tpu_custom_call" | custom-call | tf_op jit(solution)/shard_map/pallas_call | solution.py:830
  34.6 1.8 %shard_map.69 = (f32[1,4,128,128]{3,2,1,0:T(8,128)}, f32[8,4,16,128]{3,2,1,0:T(8,128)}) custom-call(f32[1,4,128,128]{3,2,1,0:T(8,128)} %get-tuple-element.4.refs_0_, f32[8,4,16,128]{3,2,1,0:T(8,128)} %get-tuple-element.5.refs_1_), custom_call_target="tpu_custom_call" | custom-call | tf_op jit(solution)/shard_map/pallas_call | solution.py:799
